TPU v7x, 512 devices: a whole 4x4x16 slice. The times are simulated.
512 devices in a mesh: grp: 16 (over z), tile: 8 (over x_hi, y), arch: 4 (over x_lo, core).
Axes of the slice: x: 4 (x_hi: 2, x_lo: 2; x = x_hi * 2 + x_lo), y: 4, z: 16, core: 2. Of those that a mesh axis runs over, the one named last changes fastest.
Arguments:
- query_grads: bfloat16 [4, 1536, 4096], P('arch', 'tile', 'grp'), may hold values from -6 to 6
- input_basis: bfloat16 [4096, 4096], P(None, 'grp'), may hold values from -0.09375 to 0.09375
- output_basis: bfloat16 [1536, 1536], P(None, 'tile'), may hold values from -0.15625 to 0.15625
- eigenvalues: float32 [1536, 4096], P('tile', 'grp'), may hold values from 0.1 to 10
- activations: bfloat16 [1024, 4096], P('arch', 'grp'), may hold values from -6 to 6
- gradients: bfloat16 [1024, 1536], P('arch', 'tile'), may hold values from -0.0099487305 to 0.0099487305
- seq_lengths: int32 [4, 8], P('arch'), may hold values from 1 to 128, 256 in all within a row
Outputs:
- preconditioned: bfloat16 [4, 4096, 1536], P('arch', 'grp', 'tile')
- sequence_scores: float32 [4, 32], P(None, 'arch')
Inputs may be any that keep to these rules, and one draw needn't show every extreme that they name: Each row of seq_lengths sums to 256, and its largest entry is exactly 128.
All inputs are finite; a program needn't handle non-finite values.
Results may differ from a plain program's by a relative error of at most 0.013.
Values may be sent and summed in bfloat16 or wider, within the bound.
A program may use at most 64 MiB of HBM per device.

v0:
```python
import jax
import jax.numpy as jnp
from jax import lax
from jax.sharding import PartitionSpec as P

damping = 0.01


def contract_first(left_side, right_side):
    return lax.dot_general(
        left_side, right_side, (((0,), (0,)), ((), ())), preferred_element_type=jnp.float32
    )


def contract_last(left_side, right_side):
    return lax.dot_general(
        left_side, right_side, (((1,), (1,)), ((), ())), preferred_element_type=jnp.float32
    )


def per_device(
    query_grads, input_basis, output_basis, eigenvalues, activations, gradients, seq_lengths
):
    local_query = query_grads[0]
    feat_rows = local_query.shape[0]
    input_cols = local_query.shape[1]
    basis_part = input_basis
    rotated_in = jnp.dot(
        lax.all_gather(local_query, "grp", axis=1, tiled=True),
        basis_part,
        preferred_element_type=jnp.float32,
    ).astype(jnp.bfloat16)
    basis_part = output_basis
    rotated = contract_first(basis_part, lax.all_gather(rotated_in, "tile", axis=0, tiled=True))
    scaled = (rotated / (eigenvalues + damping)).astype(jnp.bfloat16)
    basis_part = output_basis
    restored = lax.psum_scatter(
        jnp.dot(basis_part, scaled, preferred_element_type=jnp.float32).astype(jnp.bfloat16),
        "tile",
        scatter_dimension=0,
        tiled=True,
    )
    basis_part = input_basis
    summed = lax.psum_scatter(
        contract_last(basis_part, restored), "grp", scatter_dimension=0, tiled=True
    )
    preconditioned = summed.astype(jnp.bfloat16)
    all_queries = lax.all_gather(preconditioned[None], "arch", axis=0, tiled=True)
    query_count = all_queries.shape[0]
    stacked = jnp.transpose(all_queries, (1, 0, 2)).reshape(input_cols, query_count * feat_rows)
    projected = jnp.dot(activations, stacked, preferred_element_type=jnp.float32)
    projected = projected.reshape(activations.shape[0], query_count, feat_rows)
    partial_scores = jnp.sum(projected * gradients.astype(jnp.float32)[:, None, :], axis=2).T
    lengths = seq_lengths[0]
    ends = jnp.cumsum(lengths)
    starts = ends - lengths
    position = jnp.arange(activations.shape[0], dtype=jnp.int32)
    member = ((position[None, :] >= starts[:, None]) & (position[None, :] < ends[:, None])).astype(
        jnp.float32
    )
    seq_sizes = lengths.astype(jnp.float32)
    token_scores = lax.psum(partial_scores, ("grp", "tile"))
    totals = jnp.dot(token_scores, member.T, precision=lax.Precision.HIGHEST)
    sequence_scores = totals / seq_sizes[None, :]
    return (preconditioned[None], sequence_scores)


def solution(mesh):
    return jax.shard_map(
        per_device,
        mesh=mesh,
        in_specs=(
            P("arch", "tile", "grp"),
            P(None, "grp"),
            P(None, "tile"),
            P("tile", "grp"),
            P("arch", "grp"),
            P("arch", "tile"),
            P("arch", None),
        ),
        out_specs=(P("arch", "grp", "tile"), P(None, "arch")),
        check_vma=False,
    )
```

profile of v0, /device:TPU:24, one launch (start us, length us, event | category | flops | bytes accessed | tf_op | source)
XLA Modules:
  0.0 655.7 jit_solution(9814027762734079321)
XLA Ops:
  7.2 0.0 copy-start
  7.2 0.0 all-gather.4.cloned.1.call-start
  7.2 0.7 all-gather.4.cloned.1.call-update
  7.9 0.0 reduce-scatter.7.cloned.1.call-start
  8.0 82.1 %all-gather.4.cloned.1.call-done = bf16[1,192,4096]{2,1,0:T(8,128)(2,1)} async-done(((bf16[1,192,256]{2,1,0:T(8,128)(2,1)}), bf16[1,192,4096]{2,1,0:T(8,128)(2,1)}) %all-gather.4.cloned.1.call-update) | async-done | bytes 1572880 | tf_op jit(solution)/shard_map/all_gather | solution.py:29
  90.1 2.0 fusion.5
  92.1 35.3 %all_gather.10 = bf16[1536,256]{1,0:T(8,128)(2,1)S(1)} all-gather(bf16[192,256]{1,0:T(8,128)(2,1)S(1)} %fusion.5), channel_id=1, replica_groups=mesh['grp'=16,'tile'=8,'arch'=4] {'tile'}, dimensions={0}, use_global_device_ids=true | all-gather | bytes 884736 | tf_op jit(solution)/shard_map/all_gather | solution.py:34
  127.4 2.8 fusion
  130.2 2.3 copy.11
  132.5 0.0 reduce-scatter.7.cloned.1.call-update
  132.5 0.0 reduce-scatter.5.cloned.1.call-start
  132.6 81.9 %reduce-scatter.7.cloned.1.call-done = bf16[192,256]{1,0:T(8,128)(2,1)} async-done(((bf16[1536,256]{1,0:T(8,128)(2,1)}), bf16[192,256]{1,0:T(8,128)(2,1)}) %reduce-scatter.7.cloned.1.call-update) | async-done | bytes 98320
  214.4 3.4 convolution_bitcast_fusion
  217.8 0.0 reduce-scatter.5.cloned.1.call-update
  217.9 0.9 copy-done.4
  218.8 0.2 reduce-window.7
  219.0 75.3 %reduce-scatter.5.cloned.1.call-done = f32[256,192]{0,1:T(8,128)} async-done(((f32[4096,192]{0,1:T(8,128)}), f32[256,192]{0,1:T(8,128)}) %reduce-scatter.5.cloned.1.call-update) | async-done | bytes 196624 | tf_op jit(solution)/shard_map/reduce_scatter | solution.py:44
  294.2 1.0 convert_element_type.27
  295.2 6.7 %all-gather.1 = bf16[1024,192]{0,1:T(8,128)(2,1)S(1)} all-gather(bf16[256,192]{0,1:T(8,128)(2,1)S(1)} %convert_element_type.27), channel_id=3, replica_groups=mesh['grp'=16,'tile'=8,'arch'=4] {'arch'}, dimensions={0}, use_global_device_ids=true | all-gather | bytes 491520 | tf_op jit(solution)/shard_map/all_gather | solution.py:48
  302.0 0.3 fusion.15
  302.3 0.1 multiply_reduce_fusion
  302.3 345.4 %psum.7 = f32[4,256]{1,0:T(4,128)S(1)} all-reduce(f32[4,256]{1,0:T(4,128)S(1)} %bitcast.50), channel_id=1, replica_groups=mesh['grp'=16,'tile'=8,'arch'=4] {'grp','tile'}, use_global_device_ids=true, to_apply=%region_3.0 | all-reduce | flops 1024 | bytes 8192 | tf_op jit(solution)/shard_map/psum | solution.py:62
  647.7 0.8 convolution_divide_fusion
  648.5 0.7 convert_bitcast_fusion.1
  (14 shorter events, 0.1 us)
Async XLA Ops:
  7.2 82.9 %copy-start = (bf16[4096,256]{1,0:T(8,128)(2,1)S(1)}, bf16[4096,256]{1,0:T(8,128)(2,1)}, u32[]{:S(2)}) copy-start(bf16[4096,256]{1,0:T(8,128)(2,1)} %param.8) | copy-start | bytes 6291460
  7.2 82.9 %all-gather.4.cloned.1.call-start = ((), (), s32[]{:S(2)}) async-start(), calls=%async_computation.3 | async-start | bytes 1671168 | tf_op jit(solution)/shard_map/all_gather | solution.py:29
  7.9 119.5 %copy-start.1 = (bf16[1536,192]{0,1:T(8,128)(2,1)S(1)}, bf16[1536,192]{0,1:T(8,128)(2,1)}, u32[]{:S(2)}) copy-start(bf16[1536,192]{0,1:T(8,128)(2,1)} %param.9) | copy-start | bytes 1769476
  7.9 206.5 %reduce-scatter.7.cloned.1.call-start = ((), (), s32[]{:S(2)}) async-start(), calls=%async_computation.4 | async-start | bytes 884736
  132.5 161.7 %reduce-scatter.5.cloned.1.call-start = ((), (), s32[]{:S(2)}) async-start(), calls=%async_computation.2 | async-start | bytes 3342336 | tf_op jit(solution)/shard_map/reduce_scatter | solution.py:44
  217.8 0.9 copy-start.4
  217.8 0.9 copy-start.5
  217.8 84.1 %copy-start.3 = (bf16[256,256]{1,0:T(8,128)(2,1)S(1)}, bf16[256,256]{1,0:T(8,128)(2,1)}, u32[]{:S(2)}) copy-start(bf16[256,256]{1,0:T(8,128)(2,1)} %param.11) | copy-start | bytes 393220
  294.2 354.3 %copy-start.2 = (f32[256,192]{0,1:T(8,128)S(1)}, f32[256,192]{0,1:T(8,128)}, u32[]{:S(2)}) copy-start(f32[256,192]{0,1:T(8,128)} %reduce-scatter.5.cloned.1.call-done) | copy-start | bytes 589828
Sparse Core Ops, SparseCore 0:
  10.0 80.0 all-gather.3
  132.6 81.7 reduce-scatter.6
  218.0 76.1 reduce-scatter.4
where the time goes:
time: 667 us; the launch traced here: 656 us
  blocking collectives  387 us (58%)
  waiting for transfers between devices  240 us (36%)
  between operations  13.8 us (2%)
  matrix products  9.27 us (1%)
    psum x1, blocking collectives, per_device(): token_scores = lax.psum(partial_scores, ('grp', 'tile'))  345 us
    unnamed x4, waiting for transfers between devices  82.6 us
    all_gather x1, waiting for transfers between devices, per_device(): lax.all_gather(local_query, 'grp', axis=1, tiled=True)  82.1 us
    reduce_scatter x1, waiting for transfers between devices, per_device(): lax.psum_scatter(contract_last(basis_part, restored), 'grp', scatter_dime...  75.3 us
    all_gather x1, blocking collectives, per_device(): lax.all_gather(rotated_in, 'tile', axis=0, tiled=True)  35.3 us
  transfers between devices with their start and end apart: 3, of which 3 were waited for; matrix products, arithmetic and copies ran while one was open for 0% of the time, Pallas kernels for 0%

commit v1 on v0

v1 whole, which is shorter than its diff:
```python
import functools

import jax
import jax.numpy as jnp
from jax import lax
from jax.experimental import pallas as pl
from jax.experimental.pallas import tpu as pltpu
from jax.sharding import PartitionSpec as P

damping = 0.01
MESH = pl.DeviceIdType.MESH


def dot(a, b):
    return jnp.dot(a, b, preferred_element_type=jnp.float32)


def dot_last(a, b):
    return lax.dot_general(a, b, (((1,), (1,)), ((), ())), preferred_element_type=jnp.float32)


def kernel(
    nz, nt, na,
    q_hbm, u_hbm, vt_hbm, eig_hbm, act_hbm, gt_hbm, len_ref,
    pre_ref, score_ref,
    piece, from_left, from_right, u, vt, v, inv, gt,
    acc, rin, aprime, outgoing, arrived, rall, chain_a, chain_b, first,
    partial, seq_tile, seq_z,
    local_sem,
    zr_send, zr_recv, zl_send, zl_recv,
    t_send, t_recv, a_send, a_recv, s_send, s_recv,
    q_send, q_recv,
    rr_send, rr_recv, rl_send, rl_recv,
    pt_send, pt_recv, pz_send, pz_recv,
):
    z, t, a = lax.axis_index("grp"), lax.axis_index("tile"), lax.axis_index("arch")
    fb, db = q_hbm.shape[1], q_hbm.shape[2]
    half = fb // 2
    ra = act_hbm.shape[0] // nt
    rows = ((0, half), (half, fb - half + ra))
    reach = nz // 2
    right_reach, left_reach = (reach, reach - 1), (reach - 1, reach)

    def zdev(d):
        return {"grp": lax.rem(z + (d + nz), nz)}

    def tdev(j):
        return {"tile": lax.rem(t + j, nt)}

    def adev(j):
        return {"arch": lax.rem(a + j, na)}

    loads = [
        pltpu.make_async_copy(q_hbm.at[0], piece.at[pl.ds(0, fb)], local_sem.at[0]),
        pltpu.make_async_copy(
            act_hbm.at[pl.ds(pl.multiple_of(t * ra, ra), ra)], piece.at[pl.ds(fb, ra)], local_sem.at[1]
        ),
        pltpu.make_async_copy(u_hbm, u, local_sem.at[2]),
        pltpu.make_async_copy(vt_hbm, vt, local_sem.at[3]),
        pltpu.make_async_copy(eig_hbm, inv, local_sem.at[4]),
        pltpu.make_async_copy(gt_hbm, gt, local_sem.at[5]),
    ]
    for load in loads:
        load.start()

    barrier = pltpu.get_barrier_semaphore()
    peers = [zdev(d) for d in range(1, nz)] + [tdev(j) for j in range(1, nt)] + [adev(j) for j in range(1, na)]
    for peer in peers:
        pl.semaphore_signal(barrier, inc=1, device_id=peer, device_id_type=MESH)
    loads[0].wait()
    loads[1].wait()
    pl.semaphore_wait(barrier, len(peers))

    def remote(src, dst, send, recv, dev):
        return pltpu.make_async_remote_copy(
            src_ref=src, dst_ref=dst, send_sem=send, recv_sem=recv, device_id=dev, device_id_type=MESH
        )

    def gather_right(step, c):
        sl = pl.ds(*rows[c])
        src = piece.at[sl] if step == 0 else from_left.at[step - 1, sl]
        return remote(src, from_left.at[step, sl], zr_send.at[step, c], zr_recv.at[step, c], zdev(1))

    def gather_left(step, c):
        sl = pl.ds(*rows[c])
        src = piece.at[sl] if step == 0 else from_right.at[step - 1, sl]
        return remote(src, from_right.at[step, sl], zl_send.at[step, c], zl_recv.at[step, c], zdev(-1))

    sent = []

    def go(copy):
        copy.start()
        sent.append(copy)

    for c in range(2):
        go(gather_right(0, c))
        go(gather_left(0, c))

    def urows(d):
        k = lax.rem(z + (d + nz), nz)
        return pl.ds(pl.multiple_of(k * db, db), db)

    for load in loads[2:]:
        load.wait()
    acc[...] = dot(piece[...], u[urows(0), :])
    inv[...] = 1.0 / (inv[...] + damping)
    v[...] = vt[...].T

    def start_tile_gather(c):
        mine = pl.ds(pl.multiple_of(t * fb + c * half, 16), half)
        rin[mine, :] = acc[pl.ds(c * half, half), :].astype(jnp.bfloat16)
        for j in range(1, nt):
            go(remote(rin.at[mine], rin.at[mine], t_send.at[j, c], t_recv.at[j, c], tdev(j)))

    for step in range(reach):
        for c in range(2):
            sl = pl.ds(*rows[c])
            if step < right_reach[c]:
                gather_right(step, c).wait_recv()
                if step + 1 < right_reach[c]:
                    go(gather_right(step + 1, c))
            if step < left_reach[c]:
                gather_left(step, c).wait_recv()
                if step + 1 < left_reach[c]:
                    go(gather_left(step + 1, c))
            if step < right_reach[c]:
                acc[sl, :] += dot(from_left[step, sl, :], u[urows(-1 - step), :])
            if step < left_reach[c]:
                acc[sl, :] += dot(from_right[step, sl, :], u[urows(1 + step), :])
            if step == reach - 1:
                start_tile_gather(c)

    own_rows = pl.ds(pl.multiple_of(t * ra, ra), ra)
    aprime[own_rows, :] = acc[pl.ds(fb, ra), :].astype(jnp.bfloat16)
    for j in range(1, nt):
        go(remote(aprime.at[own_rows], aprime.at[own_rows], a_send.at[j], a_recv.at[j], tdev(j)))

    for c in range(2):
        for j in range(1, nt):
            other = lax.rem(t + (nt - j), nt)
            place = pl.ds(pl.multiple_of(other * fb + c * half, 16), half)
            remote(rin.at[place], rin.at[place], t_send.at[j, c], t_recv.at[j, c], tdev(j)).wait_recv()
    scaled = (dot(vt[...], rin[...]) * inv[...]).astype(jnp.bfloat16)

    outgoing[...] = dot(v[...], scaled).astype(jnp.bfloat16)

    def tile_scatter(j, c):
        owner = lax.rem(t + j, nt)
        src = outgoing.at[pl.ds(pl.multiple_of(owner * fb + c * half, 16), half)]
        return remote(src, arrived.at[j, pl.ds(c * half, half)], s_send.at[j, c], s_recv.at[j, c], tdev(j))

    for c in range(2):
        for j in range(1, nt):
            go(tile_scatter(j, c))

    def scatter_right(step, c):
        sl = pl.ds(c * half, half)
        src = first.at[0, sl] if step == 0 else chain_a.at[step - 1, sl]
        return remote(src, chain_a.at[step, sl], rr_send.at[step, c], rr_recv.at[step, c], zdev(1))

    def scatter_left(step, c):
        sl = pl.ds(c * half, half)
        src = first.at[1, sl] if step == 0 else chain_b.at[step - 1, sl]
        return remote(src, chain_b.at[step, sl], rl_send.at[step, c], rl_recv.at[step, c], zdev(-1))

    def share(c, d):
        return dot_last(rall[a, pl.ds(c * half, half), :], u[urows(d), :])

    for c in range(2):
        sl = pl.ds(c * half, half)
        for j in range(1, nt):
            tile_scatter(j, c).wait_recv()
        total = outgoing[pl.ds(pl.multiple_of(t * fb + c * half, 16), half), :].astype(jnp.float32)
        for j in range(1, nt):
            total += arrived[j, sl, :].astype(jnp.float32)
        rall[a, sl, :] = total.astype(jnp.bfloat16)
        first[0, sl, :] = share(c, right_reach[c]).astype(jnp.bfloat16)
        go(scatter_right(0, c))
        first[1, sl, :] = share(c, -left_reach[c]).astype(jnp.bfloat16)
        go(scatter_left(0, c))

    for j in range(1, na):
        go(remote(rall.at[a], rall.at[a], q_send.at[j], q_recv.at[j], adev(j)))

    def scores():
        for j in range(1, nt):
            other = lax.rem(t + (nt - j), nt)
            place = pl.ds(pl.multiple_of(other * ra, ra), ra)
            remote(aprime.at[place], aprime.at[place], a_send.at[j], a_recv.at[j], tdev(j)).wait_recv()
        for j in range(1, na):
            other = lax.rem(a + (na - j), na)
            remote(rall.at[other], rall.at[other], q_send.at[j], q_recv.at[j], adev(j)).wait_recv()
        position = lax.broadcasted_iota(jnp.int32, (1, nt * ra), 1)
        lane = lax.broadcasted_iota(jnp.int32, (1, 128), 1)
        weights = gt[...].astype(jnp.float32)
        seq_tile[t] = jnp.zeros((8, 128), jnp.float32)
        for q in range(na):
            token = jnp.sum(dot_last(rall[q], aprime[...]) * weights, axis=0, keepdims=True)
            line = jnp.zeros((1, 128), jnp.float32)
            start = jnp.int32(0)
            for s in range(len_ref.shape[1]):
                end = start + len_ref[0, s]
                inside = jnp.logical_and(position >= start, position < end)
                one = jnp.sum(jnp.where(inside, token, 0.0), axis=1, keepdims=True)
                line = jnp.where(lane == s, one, line)
                start = end
            seq_tile[t, pl.ds(q, 1), :] = line
        for j in range(1, nt):
            go(remote(seq_tile.at[t], seq_tile.at[t], pt_send.at[j], pt_recv.at[j], tdev(j)))

    def sum_tile():
        for j in range(1, nt):
            other = lax.rem(t + (nt - j), nt)
            remote(seq_tile.at[other], seq_tile.at[other], pt_send.at[j], pt_recv.at[j], tdev(j)).wait_recv()
        total = seq_tile[0]
        for i in range(1, nt):
            total += seq_tile[i]
        seq_z[z] = total
        for d in range(1, nz):
            go(remote(seq_z.at[z], seq_z.at[z], pz_send.at[d], pz_recv.at[d], zdev(d)))

    def sum_z():
        for d in range(1, nz):
            other = lax.rem(z + (nz - d), nz)
            remote(seq_z.at[other], seq_z.at[other], pz_send.at[d], pz_recv.at[d], zdev(d)).wait_recv()
        total = seq_z[0]
        for i in range(1, nz):
            total += seq_z[i]
        lane = lax.broadcasted_iota(jnp.int32, (1, 128), 1)
        sizes = jnp.ones((1, 128), jnp.float32)
        for s in range(len_ref.shape[1]):
            sizes = jnp.where(lane == s, len_ref[0, s].astype(jnp.float32), sizes)
        score_ref[...] = total / sizes

    for step in range(reach):
        for c in range(2):
            sl = pl.ds(c * half, half)
            if step == 0:
                partial[sl, :] = share(c, 0)
            if step < right_reach[c]:
                left_to_go = right_reach[c] - 1 - step
                if left_to_go > 0:
                    term = share(c, left_to_go)
                    scatter_right(step, c).wait_recv()
                    chain_a[step, sl, :] = (chain_a[step, sl, :].astype(jnp.float32) + term).astype(jnp.bfloat16)
                    go(scatter_right(step + 1, c))
                else:
                    scatter_right(step, c).wait_recv()
                    partial[sl, :] += chain_a[step, sl, :].astype(jnp.float32)
            if step < left_reach[c]:
                left_to_go = left_reach[c] - 1 - step
                if left_to_go > 0:
                    term = share(c, -left_to_go)
                    scatter_left(step, c).wait_recv()
                    chain_b[step, sl, :] = (chain_b[step, sl, :].astype(jnp.float32) + term).astype(jnp.bfloat16)
                    go(scatter_left(step + 1, c))
                else:
                    scatter_left(step, c).wait_recv()
                    partial[sl, :] += chain_b[step, sl, :].astype(jnp.float32)
        if step == reach // 2 - 1:
            scores()
        if step == reach - 3 or (reach < 4 and step == reach - 1):
            sum_tile()
    pre_ref[...] = partial[...].astype(jnp.bfloat16)
    sum_z()
    for copy in sent:
        copy.wait_send()


def per_device(nz, nt, na, query_grads, input_basis, output_basis, eigenvalues, activations, gradients, seq_lengths):
    fb, db = query_grads.shape[1:]
    d_all, f_all = input_basis.shape[0], output_basis.shape[0]
    archive = activations.shape[0]
    ra = archive // nt
    reach = nz // 2
    half = fb // 2
    anywhere = pl.BlockSpec(memory_space=pl.ANY)
    bf16, f32 = jnp.bfloat16, jnp.float32
    dma = pltpu.SemaphoreType.DMA
    pre, scores = pl.pallas_call(
        functools.partial(kernel, nz, nt, na),
        out_shape=(jax.ShapeDtypeStruct((fb, db), bf16), jax.ShapeDtypeStruct((8, 128), f32)),
        in_specs=[anywhere] * 6 + [pl.BlockSpec(memory_space=pltpu.SMEM)],
        out_specs=[pl.BlockSpec(memory_space=pltpu.VMEM)] * 2,
        scratch_shapes=[
            pltpu.VMEM((fb + ra, db), bf16),
            pltpu.VMEM((reach, fb + ra, db), bf16),
            pltpu.VMEM((reach, fb + ra, db), bf16),
            pltpu.VMEM((d_all, db), bf16),
            pltpu.VMEM((fb, f_all), bf16),
            pltpu.VMEM((f_all, fb), bf16),
            pltpu.VMEM((fb, db), f32),
            pltpu.VMEM((fb, archive), bf16),
            pltpu.VMEM((fb + ra, db), f32),
            pltpu.VMEM((f_all, db), bf16),
            pltpu.VMEM((archive, db), bf16),
            pltpu.VMEM((f_all, db), bf16),
            pltpu.VMEM((nt, fb, db), bf16),
            pltpu.VMEM((na, fb, db), bf16),
            pltpu.VMEM((reach, fb, db), bf16),
            pltpu.VMEM((reach, fb, db), bf16),
            pltpu.VMEM((2, fb, db), bf16),
            pltpu.VMEM((fb, db), f32),
            pltpu.VMEM((nt, 8, 128), f32),
            pltpu.VMEM((nz, 8, 128), f32),
            dma((6,)),
            dma((reach, 2)), dma((reach, 2)), dma((reach, 2)), dma((reach, 2)),
            dma((nt, 2)), dma((nt, 2)), dma((nt,)), dma((nt,)), dma((nt, 2)), dma((nt, 2)),
            dma((na,)), dma((na,)),
            dma((reach, 2)), dma((reach, 2)), dma((reach, 2)), dma((reach, 2)),
            dma((nt,)), dma((nt,)), dma((nz,)), dma((nz,)),
        ],
        compiler_params=pltpu.CompilerParams(
            collective_id=0, has_side_effects=True, vmem_limit_bytes=60 * 2**20
        ),
    )(query_grads, input_basis, output_basis.T, eigenvalues, activations, gradients.T, seq_lengths)
    return pre.T[None], scores[:na, : seq_lengths.shape[1]]


def solution(mesh):
    nz, nt, na = mesh.shape["grp"], mesh.shape["tile"], mesh.shape["arch"]
    return jax.shard_map(
        functools.partial(per_device, nz, nt, na),
        mesh=mesh,
        in_specs=(
            P("arch", "tile", "grp"),
            P(None, "grp"),
            P(None, "tile"),
            P("tile", "grp"),
            P("arch", "grp"),
            P("arch", "tile"),
            P("arch", None),
        ),
        out_specs=(P("arch", "grp", "tile"), P(None, "arch")),
        check_vma=False,
    )
```

time: 667 us -> 104 us (0.16); the launches traced: 656 us -> 103 us
  blocking collectives: 387 us -> 0 us
  waiting for transfers between devices: 240 us -> 0 us
  Pallas kernels: 0 us -> 100 us
  between operations: 13.8 us -> 0.64 us
  matrix products: 9.27 us -> 0 us
    psum x1 -> x0, blocking collectives: 345 us -> none  [per_device(): token_scores = lax.psum(partial_scores, ('grp', 'tile'))]
    pallas_call x0 -> x1, Pallas kernels: none -> 100 us  [per_device(): pl.pallas_call(functools.partial(kernel, nz, nt, na), out_shape=(jax.Shap...]
    unnamed x4 -> x0, waiting for transfers between devices: 82.6 us -> none
    all_gather x1 -> x0, waiting for transfers between devices: 82.1 us -> none  [per_device(): lax.all_gather(local_query, 'grp', axis=1, tiled=True)]
    reduce_scatter x1 -> x0, waiting for transfers between devices: 75.3 us -> none  [per_device(): lax.psum_scatter(contract_last(basis_part, restored), 'grp', scatter_dime...]
    all_gather x2 -> x0, blocking collectives: 42 us -> none  [the longest x1 35.3 us: per_device(): lax.all_gather(rotated_in, 'tile', axis=0, tiled=True)]
    dot_general x5 -> x0, matrix products: 9.27 us -> none  [the longest x1 3.39 us: contract_last(): lax.dot_general(left_side, right_side, (((1,), (1,)), ((), ())), preferre...]
  transfers between devices with their start and end apart: 3 -> 0, of which waited for: 3 -> 0; matrix products, arithmetic and copies ran while one was open for 0% -> 0% of each run, Pallas kernels for 0% -> 0%
where the time goes in v1:
time: 104 us; the launch traced here: 103 us
  Pallas kernels  100 us (96%)
  local copies, waits for them, and re-layouts  2.8 us (3%)
    pallas_call x1, Pallas kernels, per_device(): pl.pallas_call(functools.partial(kernel, nz, nt, na), out_shape=(jax.Shap...  100 us

profile of v1, /device:TPU:24, one launch (start us, length us, event | category | flops | bytes accessed | tf_op | source)
XLA Modules:
  0.0 103.4 jit_solution(6485945400040074506)
XLA Ops:
  0.6 100.0 %shard_map.86 = (bf16[192,256]{1,0:T(8,128)(2,1)}, f32[8,128]{1,0:T(8,128)}) custom-call(bf16[1,192,256]{2,1,0:T(8,128)(2,1)} %q_hbm.1, bf16[4096,256]{1,0:T(8,128)(2,1)} %u_hbm.1, bf16[192,1536]{1,0:T(8,128)(2,1)} %bitcast.5, f32[192,256]{1,0:T(8,128)} %eig_hbm.1, bf16[256,256]{1,0:T(8,128)(2,1)} %act_hbm.1, bf16[192,256]{1,0:T(8,128)(2,1)} %bitcast.7, ...), custom_call_target="tpu_custom_call" | custom-call | tf_op jit(solution)/shard_map/pallas_call | solution.py:280
  100.6 1.3 %slice.3 = f32[4,8]{1,0:T(4,128)} slice(f32[8,128]{1,0:T(8,128)} %get-tuple-element.5), slice={[0:4], [0:8]} | slice | bytes 256 | tf_op jit(solution)/shard_map/slice | solution.py:317
  101.9 1.5 %copy.10 = bf16[1,256,192]{1,2,0:T(8,128)(2,1)} copy(bf16[1,256,192]{1,2,0:T(8,128)(2,1)} %bitcast.6) | data formatting | bytes 196608

commit v2 on v0

v2 whole, which is shorter than its diff:
```python
import functools

import jax
import jax.numpy as jnp
from jax import lax
from jax.experimental import pallas as pl
from jax.experimental.pallas import tpu as pltpu
from jax.sharding import PartitionSpec as P

damping = 0.01
MESH = pl.DeviceIdType.MESH
BF16, F32 = jnp.bfloat16, jnp.float32


def dot(a, b):
    return jnp.dot(a, b, preferred_element_type=F32)


def dot_last(a, b):
    return lax.dot_general(a, b, (((1,), (1,)), ((), ())), preferred_element_type=F32)


def kernel(
    nz, nt, na,
    q_hbm, u_hbm, vt_hbm, eig_hbm, act_hbm, gt_hbm, len_ref,
    pre_ref, score_ref,
    piece, pieces, act, act_right, act_left, u, vt, v, eig, eig_pair, inv, gt,
    acc, acc_act, ybuf, rin, aprime, outgoing, arrived, restored, rall,
    first, chain, final, own, own_pair, seq_tile, seq_z,
    local_sem, f_send, g_send, g_recv, x_send, x_recv,
    ar_send, ar_recv, al_send, al_recv,
    uz_send, uz_recv, ut_send, ut_recv, uc_send, uc_recv,
    e_send, e_recv, t_send, t_recv, a_send, a_recv, s_send, s_recv,
    p_send, p_recv, q_send, q_recv,
    r0_send, r_send, r_recv, rf_recv, o_send, o_recv,
    pt_send, pt_recv, pz_send, pz_recv,
):
    z, t, a = lax.axis_index("grp"), lax.axis_index("tile"), lax.axis_index("arch")
    fb, db = q_hbm.shape[1], q_hbm.shape[2]
    part = fb // 2
    half = part // 2
    ra = act_hbm.shape[0] // nt
    d_all = u_hbm.shape[0]
    up = d_all // (2 * nt)
    reach = nz // 4
    core, pair = lax.rem(a, 2), a - lax.rem(a, 2)
    odd = lax.rem(z, 2)
    mine = pair + odd
    same = lax.rem(z + core, 2) == 0
    other_core = a + 1 - 2 * core
    z_pair = z + 1 - 2 * odd
    chunks = tuple(pl.ds(c * half, half) for c in range(2))

    def at_z(d):
        return lax.rem(z + (d + nz), nz)

    def at_tile(j):
        return lax.rem(t + j, nt)

    def remote(src, dst, send, recv, **dev):
        return pltpu.make_async_remote_copy(
            src_ref=src, dst_ref=dst, send_sem=send, recv_sem=recv, device_id=dev, device_id_type=MESH
        )

    sent = []

    def go(copy):
        copy.start()
        sent.append(copy)

    loads = [
        pltpu.make_async_copy(q_hbm.at[0], piece, local_sem.at[0]),
        pltpu.make_async_copy(act_hbm.at[pl.ds(pl.multiple_of(t * ra, ra), ra)], act, local_sem.at[1]),
        pltpu.make_async_copy(u_hbm, u.at[odd], local_sem.at[2]),
        pltpu.make_async_copy(vt_hbm, vt, local_sem.at[3]),
        pltpu.make_async_copy(eig_hbm, eig, local_sem.at[4]),
        pltpu.make_async_copy(gt_hbm, gt, local_sem.at[5]),
    ]
    for load in loads:
        load.start()

    barrier = pltpu.get_barrier_semaphore()
    peers = [{"grp": at_z(d), "arch": pair + h} for d in (1, -1) for h in (0, 1)]
    peers += [{"grp": at_z(d), "arch": pair + h} for d in (2, -2) for h in (0, 1)]
    peers += [{"tile": at_tile(j), "arch": pair + h} for j in range(1, nt) for h in (0, 1)]
    peers += [{"arch": lax.rem(a + j, na)} for j in range(1, na)]
    for peer in peers:
        pl.semaphore_signal(barrier, inc=1, device_id=peer, device_id_type=MESH)
    for load in loads:
        load.wait()
    pl.semaphore_wait(barrier, len(peers))

    def uz():
        rows = pl.ds(pl.multiple_of((2 * t + core) * up, 128), up)
        return remote(u.at[odd, rows], u.at[odd, rows], uz_send, uz_recv, grp=z_pair)

    def foreign(tile, h):
        return u.at[1 - odd, pl.ds(pl.multiple_of((2 * tile + h) * up, 128), up)]

    def ut(j):
        return remote(foreign(t, core), foreign(t, core), ut_send.at[j], ut_recv.at[j], tile=at_tile(j))

    def uc(j):
        rows = foreign(at_tile(nt - j), core)
        return remote(rows, rows, uc_send.at[j], uc_recv.at[j], arch=other_core)

    go(uz())

    hop = 2 - lax.rem(z + core, 2)
    for c in range(2):
        for h in range(2):
            src = piece.at[pl.ds(h * part + c * half, half)]
            for side, (to, slot) in enumerate(((lax.rem(z + hop, nz), nz - hop), (lax.rem(z + nz - hop, nz), hop))):
                go(remote(
                    src, pieces.at[slot, chunks[c]], f_send.at[side, h, c], g_recv.at[slot, c], grp=to, arch=pair + h
                ))

    def from_core():
        rows = pl.ds(pl.multiple_of((1 - core) * part, 16), part)
        return remote(piece.at[rows], pieces.at[0], x_send, x_recv, arch=other_core)

    @pl.when(same)
    def _():
        from_core().start()
        pieces[0] = piece[pl.ds(pl.multiple_of(core * part, 16), part), :]

    def act_hop(step, side):
        buf, send, recv, d = ((act_right, ar_send, ar_recv, 1), (act_left, al_send, al_recv, -1))[side]
        src = act if step == 0 else buf.at[step - 1]
        return remote(src, buf.at[step], send.at[step], recv.at[step], grp=at_z(d))

    act_reach = (nz // 2, nz // 2 - 1)
    go(act_hop(0, 0))
    go(act_hop(0, 1))

    def urows(d):
        return pl.ds(pl.multiple_of(at_z(d) * db, 128), db)

    def act_step(step):
        for side in range(2):
            if step < act_reach[side]:
                act_hop(step, side).wait_recv()
                if step + 1 < act_reach[side]:
                    go(act_hop(step + 1, side))
        for side, (buf, d) in enumerate(((act_right, -1 - step), (act_left, 1 + step))):
            if step < act_reach[side]:
                acc_act[...] += dot(buf[step], u[odd, urows(d), :])

    def arrive(slot, c):
        remote(piece.at[chunks[c]], pieces.at[slot, chunks[c]], g_send.at[slot, c], g_recv.at[slot, c], grp=z).wait_recv()

    def forward(slot, c, d):
        to = (slot - d) % nz
        go(remote(
            pieces.at[slot, chunks[c]], pieces.at[to, chunks[c]], g_send.at[to, c], g_recv.at[to, c], grp=at_z(d)
        ))

    acc_act[...] = dot(act[...], u[odd, urows(0), :])
    v[...] = vt[...].T

    @pl.when(jnp.logical_not(same))
    def _():
        from_core().wait_recv()

    acc[odd] = dot(pieces[0], u[odd, urows(0), :])
    ready, act_at = [0], 0
    per_step = -(-(nz // 2 - 2) // reach)
    for step in range(reach):
        new = []
        if step == reach - 1:
            for j in range(nt):
                if j:
                    ut_from = foreign(at_tile(nt - j), core)
                    remote(ut_from, ut_from, ut_send.at[j], ut_recv.at[j], tile=at_tile(j)).wait_recv()
                go(uc(j))

            @pl.when(same)
            def _():
                remote(eig, eig_pair, e_send, e_recv, grp=z_pair).start()

        for c in range(2):
            for far in (0, 1):
                for side, d in enumerate((2, -2)):
                    last = reach if far else reach - (c != side)
                    if step >= last:
                        continue
                    dist = 2 * step + (1 if far else 2)
                    slot = (-dist if side == 0 else dist) % nz
                    arrive(slot, c)
                    if step + 1 < last:
                        forward(slot, c, d)
                    if slot not in new:
                        new.append(slot)
        if step == reach - 1:
            for j in range(nt):
                rows = foreign(at_tile(nt - j), 1 - core)
                remote(rows, rows, uc_send.at[j], uc_recv.at[j], arch=other_core).wait_recv()
        else:
            if step == 0:
                uz_rows = foreign(t, core)
                remote(uz_rows, uz_rows, uz_send, uz_recv, grp=z_pair).wait_recv()
                for j in range(1, nt):
                    go(ut(j))
        for slot in new:
            acc[odd] += dot(pieces[slot], u[odd, urows(slot), :])
        ready += new
        if step < reach - 1:
            for _ in range(per_step if step else 1):
                if act_at < nz // 2 - 2:
                    act_step(act_at)
                    act_at += 1
    total = dot(pieces[0], u[1 - odd, urows(0), :])
    for slot in ready[1:]:
        total += dot(pieces[slot], u[1 - odd, urows(slot), :])
    ybuf[1 - odd] = total.astype(BF16)
    ybuf[odd] = acc[odd].astype(BF16)

    def rin_rows(tile, h):
        return pl.ds(pl.multiple_of(tile * fb + h * part, 16), part)

    def tile_gather(j, e):
        rows = rin.at[rin_rows(t, core)]
        return remote(
            ybuf.at[e], rows, t_send.at[j, e], t_recv.at[j, core], tile=at_tile(j), arch=pair + e
        )

    for j in range(1, nt):
        for e in range(2):
            go(tile_gather(j, e))
    cross = remote(
        ybuf.at[1 - core], rin.at[rin_rows(t, core)], t_send.at[0, 0], t_recv.at[0, core], arch=other_core
    )
    go(cross)
    rin[rin_rows(t, core), :] = ybuf[core]
    for step in range(act_at, nz // 2):
        act_step(step)
    own_rows = pl.ds(pl.multiple_of(t * ra, ra), ra)
    aprime[own_rows, :] = acc_act[...].astype(BF16)

    @pl.when(jnp.logical_not(same))
    def _():
        remote(eig, eig_pair, e_send, e_recv, grp=z_pair).wait_recv()
        inv[...] = 1.0 / (eig_pair[...] + damping)

    @pl.when(same)
    def _():
        inv[...] = 1.0 / (eig[...] + damping)

    def tile_wait(j, h):
        rows = rin.at[rin_rows(at_tile(nt - j), h)]
        remote(rows, rows, t_send.at[j, 0], t_recv.at[j, h], arch=other_core).wait_recv()

    tile_wait(0, 1 - core)
    for j in range(1, nt):
        for h in range(2):
            tile_wait(j, h)
    scaled = (dot(vt[...], rin[...]) * inv[...]).astype(BF16)

    outgoing[...] = dot(v[...], scaled).astype(BF16)

    def tile_scatter(j, h):
        src = outgoing.at[rin_rows(at_tile(j), h)]
        return remote(src, arrived.at[j, core], s_send.at[j, h], s_recv.at[j, core], tile=at_tile(j), arch=pair + h)

    for j in range(1, nt):
        for h in range(2):
            go(tile_scatter(j, h))
    go(remote(
        outgoing.at[rin_rows(t, 1 - core)], arrived.at[0, core], s_send.at[0, 0], s_recv.at[0, core], arch=other_core
    ))
    arrived[0, core] = outgoing[rin_rows(t, core), :]
    for j in range(1, nt):
        go(remote(aprime.at[own_rows], aprime.at[own_rows], a_send.at[j], a_recv.at[j], tile=at_tile(j)))

    def scatter_wait(j, e):
        dst = arrived.at[j, e]
        remote(dst, dst, s_send.at[j, 0], s_recv.at[j, e], arch=other_core).wait_recv()

    scatter_wait(0, 1 - core)
    for j in range(1, nt):
        for e in range(2):
            scatter_wait(j, e)
    for e in range(2):
        total = arrived[0, e].astype(F32)
        for j in range(1, nt):
            total += arrived[j, e].astype(F32)
        restored[e] = total.astype(BF16)

    def share(d):
        rows = urows(d)
        return dot_last(restored[0], u[0, rows, :]) + dot_last(restored[1], u[1, rows, :])

    def lasts(far, side):
        return tuple(reach if far else reach - (c != side) for c in range(2))

    def scatter(step, c, far, side):
        last = lasts(far, side)[c]
        src = first.at[far, side, chunks[c]] if step == 0 else chain.at[far, side, step - 1, chunks[c]]
        d = 2 if side == 0 else -2
        if step < last - 1:
            return remote(
                src, chain.at[far, side, step, chunks[c]], r_send.at[far, side, step, c],
                r_recv.at[far, side, step, c], grp=at_z(d),
            )
        return remote(
            src, final.at[side, core, chunks[c]], r0_send.at[far, side, c], rf_recv.at[side, core, c],
            grp=at_z(d // 2 if far else d), arch=mine,
        )

    def distance(step, c, far, side):
        m = 2 * (lasts(far, side)[c] - step) - far
        return m if side == 0 else -m

    for far in (0, 1):
        for side in range(2):
            terms = {}
            for c in range(2):
                m = distance(0, c, far, side)
                if m not in terms:
                    terms[m] = share(m)
                first[far, side, chunks[c], :] = terms[m][c * half:(c + 1) * half].astype(BF16)
                go(scatter(0, c, far, side))

    core_rows = pl.ds(pl.multiple_of(core * part, 16), part)
    rall[mine, core_rows, :] = restored[odd]
    go(remote(restored.at[1 - odd], rall.at[mine, core_rows], p_send, p_recv, grp=z_pair))
    for j in range(1, na):
        go(remote(
            rall.at[mine, core_rows], rall.at[mine, core_rows], q_send.at[j, 0], q_recv.at[j, 0], arch=lax.rem(a + j, na)
        ))

    def spread():
        slot = rall.at[pair + 1 - odd, core_rows]
        remote(slot, slot, p_send, p_recv, grp=z_pair).wait_recv()
        for j in range(1, na):
            go(remote(slot, slot, q_send.at[j, 1], q_recv.at[j, 1], arch=lax.rem(a + j, na)))

    def scores():
        for j in range(1, nt):
            place = aprime.at[pl.ds(pl.multiple_of(at_tile(nt - j) * ra, ra), ra)]
            remote(place, place, a_send.at[j], a_recv.at[j], tile=at_tile(j)).wait_recv()
        for j in range(1, na):
            src = lax.rem(a + (na - j), na)
            src_core = lax.rem(src, 2)
            rows = pl.ds(pl.multiple_of(src_core * part, 16), part)
            for which, q in enumerate((src - src_core + odd, src - src_core + 1 - odd)):
                slot = rall.at[q, rows]
                remote(slot, slot, q_send.at[j, which], q_recv.at[j, which], arch=src).wait_recv()
        position = lax.broadcasted_iota(jnp.int32, (1, nt * ra), 1)
        lane = lax.broadcasted_iota(jnp.int32, (1, 128), 1)
        weights = gt[...].astype(F32)
        seq_tile[t] = jnp.zeros((8, 128), F32)
        for q in range(na):
            token = jnp.sum(dot_last(rall[q], aprime[...]) * weights, axis=0, keepdims=True)
            line = jnp.zeros((1, 128), F32)
            start = jnp.int32(0)
            for s in range(len_ref.shape[1]):
                end = start + len_ref[0, s]
                inside = jnp.logical_and(position >= start, position < end)
                one = jnp.sum(jnp.where(inside, token, 0.0), axis=1, keepdims=True)
                line = jnp.where(lane == s, one, line)
                start = end
            seq_tile[t, pl.ds(q, 1), :] = line
        for j in range(1, nt):
            go(remote(seq_tile.at[t], seq_tile.at[t], pt_send.at[j], pt_recv.at[j], tile=at_tile(j)))

    def sum_tile():
        for j in range(1, nt):
            slot = seq_tile.at[at_tile(nt - j)]
            remote(slot, slot, pt_send.at[j], pt_recv.at[j], tile=at_tile(j)).wait_recv()
        total = seq_tile[0]
        for i in range(1, nt):
            total += seq_tile[i]
        seq_z[z] = total
        for d in range(1, nz):
            go(remote(seq_z.at[z], seq_z.at[z], pz_send.at[d], pz_recv.at[d], grp=at_z(d)))

    def sum_z():
        for d in range(1, nz):
            slot = seq_z.at[at_z(-d)]
            remote(slot, slot, pz_send.at[d], pz_recv.at[d], grp=at_z(d)).wait_recv()
        total = seq_z[0]
        for i in range(1, nz):
            total += seq_z[i]
        lane = lax.broadcasted_iota(jnp.int32, (1, 128), 1)
        sizes = jnp.ones((1, 128), F32)
        for s in range(len_ref.shape[1]):
            sizes = jnp.where(lane == s, len_ref[0, s].astype(F32), sizes)
        score_ref[...] = total / sizes

    for step in range(1, reach):
        for far in (0, 1):
            for side in range(2):
                terms = {}
                for c in range(2):
                    if step < lasts(far, side)[c]:
                        m = distance(step, c, far, side)
                        if m not in terms:
                            terms[m] = share(m)
                for c in range(2):
                    if step >= lasts(far, side)[c]:
                        continue
                    m = distance(step, c, far, side)
                    scatter(step - 1, c, far, side).wait_recv()
                    got = chain[far, side, step - 1, chunks[c], :].astype(F32)
                    chain[far, side, step - 1, chunks[c], :] = (
                        got + terms[m][c * half:(c + 1) * half]
                    ).astype(BF16)
                    go(scatter(step, c, far, side))
        if step == 1:
            own[...] = share(0)

            @pl.when(jnp.logical_not(same))
            def _():
                own_pair[0] = own[...].astype(BF16)
                remote(own_pair.at[0], own_pair.at[1], o_send, o_recv, arch=other_core).start()

            spread()
        if step == max(reach - 2, 1):
            scores()
        if step == reach - 1:
            sum_tile()

    for side in range(2):
        for h in range(2):
            for c in range(2):
                slot = final.at[side, h, chunks[c]]
                remote(slot, slot, r0_send.at[0, side, c], rf_recv.at[side, h, c], grp=z_pair).wait_recv()
    for h in range(2):
        total = final[0, h].astype(F32) + final[1, h].astype(F32)
        pre_ref[pl.ds(h * part, part), :] = total.astype(BF16)

    @pl.when(same)
    def _():
        remote(own_pair.at[0], own_pair.at[1], o_send, o_recv, arch=other_core).wait_recv()
        for h, term in ((core, own[...]), (1 - core, own_pair[1].astype(F32))):
            total = final[0, h].astype(F32) + final[1, h].astype(F32) + term
            pre_ref[pl.ds(pl.multiple_of(h * part, 16), part), :] = total.astype(BF16)

    sum_z()
    for copy in sent:
        copy.wait_send()

    @pl.when(same)
    def _():
        from_core().wait_send()
        remote(eig, eig_pair, e_send, e_recv, grp=z_pair).wait_send()

    @pl.when(jnp.logical_not(same))
    def _():
        remote(own_pair.at[0], own_pair.at[1], o_send, o_recv, arch=other_core).wait_send()


def per_device(nz, nt, na, query_grads, input_basis, output_basis, eigenvalues, activations, gradients, seq_lengths):
    fb, db = query_grads.shape[1:]
    d_all, f_all = input_basis.shape[0], output_basis.shape[0]
    archive = activations.shape[0]
    ra = archive // nt
    part = fb // 2
    reach = nz // 4
    anywhere = pl.BlockSpec(memory_space=pl.ANY)
    dma = pltpu.SemaphoreType.DMA
    vmem = pltpu.VMEM
    one = dma(())
    pre, scores = pl.pallas_call(
        functools.partial(kernel, nz, nt, na),
        out_shape=(jax.ShapeDtypeStruct((fb, db), BF16), jax.ShapeDtypeStruct((8, 128), F32)),
        in_specs=[anywhere] * 6 + [pl.BlockSpec(memory_space=pltpu.SMEM)],
        out_specs=[pl.BlockSpec(memory_space=pltpu.VMEM)] * 2,
        scratch_shapes=[
            vmem((fb, db), BF16),
            vmem((nz, part, db), BF16),
            vmem((ra, db), BF16),
            vmem((nz // 2, ra, db), BF16),
            vmem((nz // 2, ra, db), BF16),
            vmem((2, d_all, db), BF16),
            vmem((fb, f_all), BF16),
            vmem((f_all, fb), BF16),
            vmem((fb, db), F32),
            vmem((fb, db), F32),
            vmem((fb, db), F32),
            vmem((fb, archive), BF16),
            vmem((2, part, db), F32),
            vmem((ra, db), F32),
            vmem((2, part, db), BF16),
            vmem((f_all, db), BF16),
            vmem((archive, db), BF16),
            vmem((f_all, db), BF16),
            vmem((nt, 2, part, db), BF16),
            vmem((2, part, db), BF16),
            vmem((na, fb, db), BF16),
            vmem((2, 2, part, db), BF16),
            vmem((2, 2, reach, part, db), BF16),
            vmem((2, 2, part, db), BF16),
            vmem((part, db), F32),
            vmem((2, part, db), BF16),
            vmem((nt, 8, 128), F32),
            vmem((nz, 8, 128), F32),
            dma((6,)), dma((2, 2, 2)), dma((nz, 2)), dma((nz, 2)), one, one,
            dma((nz // 2,)), dma((nz // 2,)), dma((nz // 2,)), dma((nz // 2,)),
            one, one, dma((nt,)), dma((nt,)), dma((nt,)), dma((nt,)),
            one, one, dma((nt, 2)), dma((nt, 2)), dma((nt,)), dma((nt,)), dma((nt, 2)), dma((nt, 2)),
            one, one, dma((na, 2)), dma((na, 2)),
            dma((2, 2, 2)), dma((2, 2, reach, 2)), dma((2, 2, reach, 2)), dma((2, 2, 2)), one, one,
            dma((nt,)), dma((nt,)), dma((nz,)), dma((nz,)),
        ],
        compiler_params=pltpu.CompilerParams(
            collective_id=0, has_side_effects=True, vmem_limit_bytes=60 * 2**20
        ),
    )(query_grads, input_basis, output_basis.T, eigenvalues, activations, gradients.T, seq_lengths)
    return pre.T[None], scores[:na, : seq_lengths.shape[1]]


def solution(mesh):
    nz, nt, na = mesh.shape["grp"], mesh.shape["tile"], mesh.shape["arch"]
    return jax.shard_map(
        functools.partial(per_device, nz, nt, na),
        mesh=mesh,
        in_specs=(
            P("arch", "tile", "grp"),
            P(None, "grp"),
            P(None, "tile"),
            P("tile", "grp"),
            P("arch", "grp"),
            P("arch", "tile"),
            P("arch", None),
        ),
        out_specs=(P("arch", "grp", "tile"), P(None, "arch")),
        check_vma=False,
    )
```

time: 667 us -> 102 us (0.15); the launches traced: 656 us -> 101 us
  blocking collectives: 387 us -> 0 us
  waiting for transfers between devices: 240 us -> 0 us
  Pallas kernels: 0 us -> 98 us
  between operations: 13.8 us -> 0.64 us
  matrix products: 9.27 us -> 0 us
    psum x1 -> x0, blocking collectives: 345 us -> none  [per_device(): token_scores = lax.psum(partial_scores, ('grp', 'tile'))]
    pallas_call x0 -> x1, Pallas kernels: none -> 98 us  [per_device(): pl.pallas_call(functools.partial(kernel, nz, nt, na), out_shape=(jax.Shap...]
    unnamed x4 -> x0, waiting for transfers between devices: 82.6 us -> none
    all_gather x1 -> x0, waiting for transfers between devices: 82.1 us -> none  [per_device(): lax.all_gather(local_query, 'grp', axis=1, tiled=True)]
    reduce_scatter x1 -> x0, waiting for transfers between devices: 75.3 us -> none  [per_device(): lax.psum_scatter(contract_last(basis_part, restored), 'grp', scatter_dime...]
    all_gather x2 -> x0, blocking collectives: 42 us -> none  [the longest x1 35.3 us: per_device(): lax.all_gather(rotated_in, 'tile', axis=0, tiled=True)]
    dot_general x5 -> x0, matrix products: 9.27 us -> none  [the longest x1 3.39 us: contract_last(): lax.dot_general(left_side, right_side, (((1,), (1,)), ((), ())), preferre...]
  transfers between devices with their start and end apart: 3 -> 0, of which waited for: 3 -> 0; matrix products, arithmetic and copies ran while one was open for 0% -> 0% of each run, Pallas kernels for 0% -> 0%
where the time goes in v2:
time: 102 us; the launch traced here: 101 us
  Pallas kernels  98 us (96%)
  local copies, waits for them, and re-layouts  2.8 us (3%)
    pallas_call x1, Pallas kernels, per_device(): pl.pallas_call(functools.partial(kernel, nz, nt, na), out_shape=(jax.Shap...  98 us

profile of v2, /device:TPU:24, one launch (start us, length us, event | category | flops | bytes accessed | tf_op | source)
XLA Modules:
  0.0 101.4 jit_solution(18279321117212174390)
XLA Ops:
  0.6 98.0 %shard_map.86 = (bf16[192,256]{1,0:T(8,128)(2,1)}, f32[8,128]{1,0:T(8,128)}) custom-call(bf16[1,192,256]{2,1,0:T(8,128)(2,1)} %q_hbm.1, bf16[4096,256]{1,0:T(8,128)(2,1)} %u_hbm.1, bf16[192,1536]{1,0:T(8,128)(2,1)} %bitcast.5, f32[192,256]{1,0:T(8,128)} %eig_hbm.1, bf16[256,256]{1,0:T(8,128)(2,1)} %act_hbm.1, bf16[192,256]{1,0:T(8,128)(2,1)} %bitcast.7, ...), custom_call_target="tpu_custom_call" | custom-call | tf_op jit(solution)/shard_map/pallas_call | solution.py:465
  98.6 1.3 %slice.3 = f32[4,8]{1,0:T(4,128)} slice(f32[8,128]{1,0:T(8,128)} %get-tuple-element.5), slice={[0:4], [0:8]} | slice | bytes 256 | tf_op jit(solution)/shard_map/slice | solution.py:511
  99.9 1.5 %copy.10 = bf16[1,256,192]{1,2,0:T(8,128)(2,1)} copy(bf16[1,256,192]{1,2,0:T(8,128)(2,1)} %bitcast.6) | data formatting | bytes 196608

commit v3 on v2

--- a/solution.py
+++ b/solution.py
@@ -24,11 +24,11 @@
     nz, nt, na,
     q_hbm, u_hbm, vt_hbm, eig_hbm, act_hbm, gt_hbm, len_ref,
     pre_ref, score_ref,
-    piece, pieces, act, act_right, act_left, u, vt, v, eig, eig_pair, inv, gt,
-    acc, acc_act, ybuf, rin, aprime, outgoing, arrived, restored, rall,
-    first, chain, final, own, own_pair, seq_tile, seq_z,
+    piece, pieces, act, acts, u, vt, v, eig, eig_pair, inv, gt,
+    acc, ybuf, rin, aprime, outgoing, arrived, restored, rall,
+    first, chain, final, own, own_pair, tokens, seq_tile, seq_z,
     local_sem, f_send, g_send, g_recv, x_send, x_recv,
-    ar_send, ar_recv, al_send, al_recv,
+    ar_send, ar_recv,
     uz_send, uz_recv, ut_send, ut_recv, uc_send, uc_recv,
     e_send, e_recv, t_send, t_recv, a_send, a_recv, s_send, s_recv,
     p_send, p_recv, q_send, q_recv,
@@ -86,8 +86,7 @@
     peers += [{"arch": lax.rem(a + j, na)} for j in range(1, na)]
     for peer in peers:
         pl.semaphore_signal(barrier, inc=1, device_id=peer, device_id_type=MESH)
-    for load in loads:
-        load.wait()
+    loads[0].wait()
     pl.semaphore_wait(barrier, len(peers))
 
     def uz():
@@ -103,8 +102,6 @@
     def uc(j):
         rows = foreign(at_tile(nt - j), core)
         return remote(rows, rows, uc_send.at[j], uc_recv.at[j], arch=other_core)
-
-    go(uz())
 
     hop = 2 - lax.rem(z + core, 2)
     for c in range(2):
@@ -124,27 +121,24 @@
         from_core().start()
         pieces[0] = piece[pl.ds(pl.multiple_of(core * part, 16), part), :]
 
-    def act_hop(step, side):
-        buf, send, recv, d = ((act_right, ar_send, ar_recv, 1), (act_left, al_send, al_recv, -1))[side]
-        src = act if step == 0 else buf.at[step - 1]
-        return remote(src, buf.at[step], send.at[step], recv.at[step], grp=at_z(d))
-
-    act_reach = (nz // 2, nz // 2 - 1)
-    go(act_hop(0, 0))
-    go(act_hop(0, 1))
+    loads[2].wait()
+    go(uz())
+    for load in (loads[1], *loads[3:]):
+        load.wait()
 
     def urows(d):
         return pl.ds(pl.multiple_of(at_z(d) * db, 128), db)
 
-    def act_step(step):
-        for side in range(2):
-            if step < act_reach[side]:
-                act_hop(step, side).wait_recv()
-                if step + 1 < act_reach[side]:
-                    go(act_hop(step + 1, side))
-        for side, (buf, d) in enumerate(((act_right, -1 - step), (act_left, 1 + step))):
-            if step < act_reach[side]:
-                acc_act[...] += dot(buf[step], u[odd, urows(d), :])
+    own_rows = pl.ds(pl.multiple_of(t * ra, ra), ra)
+
+    def act_product():
+        total = dot(act[...], u[odd, urows(0), :])
+        for d in range(1, nz):
+            remote(act, acts.at[d], ar_send.at[d], ar_recv.at[d], grp=at_z(d)).wait_recv()
+            total += dot(acts[d], u[odd, urows(-d), :])
+        aprime[own_rows, :] = total.astype(BF16)
+        for j in range(1, nt):
+            go(remote(aprime.at[own_rows], aprime.at[own_rows], a_send.at[j], a_recv.at[j], tile=at_tile(j)))
 
     def arrive(slot, c):
         remote(piece.at[chunks[c]], pieces.at[slot, chunks[c]], g_send.at[slot, c], g_recv.at[slot, c], grp=z).wait_recv()
@@ -155,7 +149,6 @@
             pieces.at[slot, chunks[c]], pieces.at[to, chunks[c]], g_send.at[to, c], g_recv.at[to, c], grp=at_z(d)
         ))
 
-    acc_act[...] = dot(act[...], u[odd, urows(0), :])
     v[...] = vt[...].T
 
     @pl.when(jnp.logical_not(same))
@@ -163,8 +156,7 @@
         from_core().wait_recv()
 
     acc[odd] = dot(pieces[0], u[odd, urows(0), :])
-    ready, act_at = [0], 0
-    per_step = -(-(nz // 2 - 2) // reach)
+    ready = [0]
     for step in range(reach):
         new = []
         if step == reach - 1:
@@ -204,11 +196,6 @@
         for slot in new:
             acc[odd] += dot(pieces[slot], u[odd, urows(slot), :])
         ready += new
-        if step < reach - 1:
-            for _ in range(per_step if step else 1):
-                if act_at < nz // 2 - 2:
-                    act_step(act_at)
-                    act_at += 1
     total = dot(pieces[0], u[1 - odd, urows(0), :])
     for slot in ready[1:]:
         total += dot(pieces[slot], u[1 - odd, urows(slot), :])
@@ -232,10 +219,8 @@
     )
     go(cross)
     rin[rin_rows(t, core), :] = ybuf[core]
-    for step in range(act_at, nz // 2):
-        act_step(step)
-    own_rows = pl.ds(pl.multiple_of(t * ra, ra), ra)
-    aprime[own_rows, :] = acc_act[...].astype(BF16)
+    for d in sorted(range(1, nz), key=lambda k: -min(k, nz - k)):
+        go(remote(act, acts.at[d], ar_send.at[d], ar_recv.at[d], grp=at_z(d)))
 
     @pl.when(jnp.logical_not(same))
     def _():
@@ -269,8 +254,6 @@
         outgoing.at[rin_rows(t, 1 - core)], arrived.at[0, core], s_send.at[0, 0], s_recv.at[0, core], arch=other_core
     ))
     arrived[0, core] = outgoing[rin_rows(t, core), :]
-    for j in range(1, nt):
-        go(remote(aprime.at[own_rows], aprime.at[own_rows], a_send.at[j], a_recv.at[j], tile=at_tile(j)))
 
     def scatter_wait(j, e):
         dst = arrived.at[j, e]
@@ -311,6 +294,14 @@
         m = 2 * (lasts(far, side)[c] - step) - far
         return m if side == 0 else -m
 
+    core_rows = pl.ds(pl.multiple_of(core * part, 16), part)
+    rall[mine, core_rows, :] = restored[odd]
+    go(remote(restored.at[1 - odd], rall.at[mine, core_rows], p_send, p_recv, grp=z_pair))
+    for j in range(1, na):
+        go(remote(
+            rall.at[mine, core_rows], rall.at[mine, core_rows], q_send.at[j, 0], q_recv.at[j, 0], arch=lax.rem(a + j, na)
+        ))
+
     for far in (0, 1):
         for side in range(2):
             terms = {}
@@ -321,13 +312,7 @@
                 first[far, side, chunks[c], :] = terms[m][c * half:(c + 1) * half].astype(BF16)
                 go(scatter(0, c, far, side))
 
-    core_rows = pl.ds(pl.multiple_of(core * part, 16), part)
-    rall[mine, core_rows, :] = restored[odd]
-    go(remote(restored.at[1 - odd], rall.at[mine, core_rows], p_send, p_recv, grp=z_pair))
-    for j in range(1, na):
-        go(remote(
-            rall.at[mine, core_rows], rall.at[mine, core_rows], q_send.at[j, 0], q_recv.at[j, 0], arch=lax.rem(a + j, na)
-        ))
+    act_product()
 
     def spread():
         slot = rall.at[pair + 1 - odd, core_rows]
@@ -335,32 +320,30 @@
         for j in range(1, na):
             go(remote(slot, slot, q_send.at[j, 1], q_recv.at[j, 1], arch=lax.rem(a + j, na)))
 
-    def scores():
-        for j in range(1, nt):
-            place = aprime.at[pl.ds(pl.multiple_of(at_tile(nt - j) * ra, ra), ra)]
-            remote(place, place, a_send.at[j], a_recv.at[j], tile=at_tile(j)).wait_recv()
+    def token(q):
+        product = dot_last(rall[q], aprime[...]) * gt[...].astype(F32)
+        tokens[pl.ds(q, 1), :] = jnp.sum(product, axis=0, keepdims=True)
+
+    def arch_wait(which):
         for j in range(1, na):
             src = lax.rem(a + (na - j), na)
             src_core = lax.rem(src, 2)
-            rows = pl.ds(pl.multiple_of(src_core * part, 16), part)
-            for which, q in enumerate((src - src_core + odd, src - src_core + 1 - odd)):
-                slot = rall.at[q, rows]
-                remote(slot, slot, q_send.at[j, which], q_recv.at[j, which], arch=src).wait_recv()
-        position = lax.broadcasted_iota(jnp.int32, (1, nt * ra), 1)
-        lane = lax.broadcasted_iota(jnp.int32, (1, 128), 1)
-        weights = gt[...].astype(F32)
-        seq_tile[t] = jnp.zeros((8, 128), F32)
-        for q in range(na):
-            token = jnp.sum(dot_last(rall[q], aprime[...]) * weights, axis=0, keepdims=True)
-            line = jnp.zeros((1, 128), F32)
-            start = jnp.int32(0)
-            for s in range(len_ref.shape[1]):
-                end = start + len_ref[0, s]
-                inside = jnp.logical_and(position >= start, position < end)
-                one = jnp.sum(jnp.where(inside, token, 0.0), axis=1, keepdims=True)
-                line = jnp.where(lane == s, one, line)
-                start = end
-            seq_tile[t, pl.ds(q, 1), :] = line
+            q = src - src_core + (odd if which == 0 else 1 - odd)
+            slot = rall.at[q, pl.ds(pl.multiple_of(src_core * part, 16), part)]
+            remote(slot, slot, q_send.at[j, which], q_recv.at[j, which], arch=src).wait_recv()
+
+    def scores():
+        position = lax.broadcasted_iota(jnp.int32, (8, nt * ra), 1)
+        lane = lax.broadcasted_iota(jnp.int32, (8, 128), 1)
+        line = jnp.zeros((8, 128), F32)
+        start = jnp.int32(0)
+        for s in range(len_ref.shape[1]):
+            end = start + len_ref[0, s]
+            inside = jnp.logical_and(position >= start, position < end)
+            one = jnp.sum(jnp.where(inside, tokens[...], 0.0), axis=1, keepdims=True)
+            line = jnp.where(lane == s, one, line)
+            start = end
+        seq_tile[t] = line
         for j in range(1, nt):
             go(remote(seq_tile.at[t], seq_tile.at[t], pt_send.at[j], pt_recv.at[j], tile=at_tile(j)))
 
@@ -388,6 +371,7 @@
             sizes = jnp.where(lane == s, len_ref[0, s].astype(F32), sizes)
         score_ref[...] = total / sizes
 
+    spread()
     for step in range(1, reach):
         for far in (0, 1):
             for side in range(2):
@@ -415,12 +399,21 @@
                 own_pair[0] = own[...].astype(BF16)
                 remote(own_pair.at[0], own_pair.at[1], o_send, o_recv, arch=other_core).start()
 
-            spread()
-        if step == max(reach - 2, 1):
+            tokens[...] = jnp.zeros_like(tokens)
+            for j in range(1, nt):
+                place = aprime.at[pl.ds(pl.multiple_of(at_tile(nt - j) * ra, ra), ra)]
+                remote(place, place, a_send.at[j], a_recv.at[j], tile=at_tile(j)).wait_recv()
+            for which in range(2):
+                arch_wait(which)
+                q = odd if which == 0 else 1 - odd
+                token(q)
+                token(2 + q)
             scores()
-        if step == reach - 1:
+        if step == max(reach - 2, 2):
             sum_tile()
 
+    if reach == 2:
+        sum_tile()
     for side in range(2):
         for h in range(2):
             for c in range(2):
@@ -471,8 +464,7 @@
             vmem((fb, db), BF16),
             vmem((nz, part, db), BF16),
             vmem((ra, db), BF16),
-            vmem((nz // 2, ra, db), BF16),
-            vmem((nz // 2, ra, db), BF16),
+            vmem((nz, ra, db), BF16),
             vmem((2, d_all, db), BF16),
             vmem((fb, f_all), BF16),
             vmem((f_all, fb), BF16),
@@ -481,7 +473,6 @@
             vmem((fb, db), F32),
             vmem((fb, archive), BF16),
             vmem((2, part, db), F32),
-            vmem((ra, db), F32),
             vmem((2, part, db), BF16),
             vmem((f_all, db), BF16),
             vmem((archive, db), BF16),
@@ -494,10 +485,11 @@
             vmem((2, 2, part, db), BF16),
             vmem((part, db), F32),
             vmem((2, part, db), BF16),
+            vmem((8, archive), F32),
             vmem((nt, 8, 128), F32),
             vmem((nz, 8, 128), F32),
             dma((6,)), dma((2, 2, 2)), dma((nz, 2)), dma((nz, 2)), one, one,
-            dma((nz // 2,)), dma((nz // 2,)), dma((nz // 2,)), dma((nz // 2,)),
+            dma((nz,)), dma((nz,)),
             one, one, dma((nt,)), dma((nt,)), dma((nt,)), dma((nt,)),
             one, one, dma((nt, 2)), dma((nt, 2)), dma((nt,)), dma((nt,)), dma((nt, 2)), dma((nt, 2)),
             one, one, dma((na, 2)), dma((na, 2)),

time: 102 us -> 97.3 us (0.954)
  Pallas kernels: 98 us -> 93.6 us
    pallas_call x1, Pallas kernels: 98 us -> 93.6 us  [per_device(): pl.pallas_call(functools.partial(kernel, nz, nt, na), out_shape=(jax.Shap...]
where the time goes in v3:
time: 97.3 us; the launch traced here: 97.1 us
  Pallas kernels  93.6 us (96%)
  local copies, waits for them, and re-layouts  2.8 us (3%)
    pallas_call x1, Pallas kernels, per_device(): pl.pallas_call(functools.partial(kernel, nz, nt, na), out_shape=(jax.Shap...  93.6 us

profile of v3, /device:TPU:24, one launch (start us, length us, event | category | flops | bytes accessed | tf_op | source)
XLA Modules:
  0.0 97.1 jit_solution(5110584607102308200)
XLA Ops:
  0.6 93.6 %shard_map.86 = (bf16[192,256]{1,0:T(8,128)(2,1)}, f32[8,128]{1,0:T(8,128)}) custom-call(bf16[1,192,256]{2,1,0:T(8,128)(2,1)} %q_hbm.1, bf16[4096,256]{1,0:T(8,128)(2,1)} %u_hbm.1, bf16[192,1536]{1,0:T(8,128)(2,1)} %bitcast.5, f32[192,256]{1,0:T(8,128)} %eig_hbm.1, bf16[256,256]{1,0:T(8,128)(2,1)} %act_hbm.1, bf16[192,256]{1,0:T(8,128)(2,1)} %bitcast.7, ...), custom_call_target="tpu_custom_call" | custom-call | tf_op jit(solution)/shard_map/pallas_call | solution.py:458
  94.3 1.3 %slice.3 = f32[4,8]{1,0:T(4,128)} slice(f32[8,128]{1,0:T(8,128)} %get-tuple-element.5), slice={[0:4], [0:8]} | slice | bytes 256 | tf_op jit(solution)/shard_map/slice | solution.py:503
  95.5 1.5 %copy.10 = bf16[1,256,192]{1,2,0:T(8,128)(2,1)} copy(bf16[1,256,192]{1,2,0:T(8,128)(2,1)} %bitcast.6) | data formatting | bytes 196608

commit v4 on v3

--- a/solution.py
+++ b/solution.py
@@ -38,7 +38,8 @@
     z, t, a = lax.axis_index("grp"), lax.axis_index("tile"), lax.axis_index("arch")
     fb, db = q_hbm.shape[1], q_hbm.shape[2]
     part = fb // 2
-    half = part // 2
+    nc = 2
+    half = part // nc
     ra = act_hbm.shape[0] // nt
     d_all = u_hbm.shape[0]
     up = d_all // (2 * nt)
@@ -49,7 +50,7 @@
     same = lax.rem(z + core, 2) == 0
     other_core = a + 1 - 2 * core
     z_pair = z + 1 - 2 * odd
-    chunks = tuple(pl.ds(c * half, half) for c in range(2))
+    chunks = tuple(pl.ds(c * half, half) for c in range(nc))
 
     def at_z(d):
         return lax.rem(z + (d + nz), nz)
@@ -63,6 +64,7 @@
         )
 
     sent = []
+    far_first = sorted(range(1, nt), key=lambda j: -(2 * (j >= nt // 2) + min(j % (nt // 2), nt // 2 - j % (nt // 2))))
 
     def go(copy):
         copy.start()
@@ -104,7 +106,7 @@
         return remote(rows, rows, uc_send.at[j], uc_recv.at[j], arch=other_core)
 
     hop = 2 - lax.rem(z + core, 2)
-    for c in range(2):
+    for c in range(nc):
         for h in range(2):
             src = piece.at[pl.ds(h * part + c * half, half)]
             for side, (to, slot) in enumerate(((lax.rem(z + hop, nz), nz - hop), (lax.rem(z + nz - hop, nz), hop))):
@@ -170,10 +172,10 @@
             def _():
                 remote(eig, eig_pair, e_send, e_recv, grp=z_pair).start()
 
-        for c in range(2):
+        for c in range(nc):
             for far in (0, 1):
                 for side, d in enumerate((2, -2)):
-                    last = reach if far else reach - (c != side)
+                    last = reach if far else reach - (c % 2 != side)
                     if step >= last:
                         continue
                     dist = 2 * step + (1 if far else 2)
@@ -211,7 +213,7 @@
             ybuf.at[e], rows, t_send.at[j, e], t_recv.at[j, core], tile=at_tile(j), arch=pair + e
         )
 
-    for j in range(1, nt):
+    for j in far_first:
         for e in range(2):
             go(tile_gather(j, e))
     cross = remote(
@@ -241,15 +243,19 @@
             tile_wait(j, h)
     scaled = (dot(vt[...], rin[...]) * inv[...]).astype(BF16)
 
-    outgoing[...] = dot(v[...], scaled).astype(BF16)
-
     def tile_scatter(j, h):
         src = outgoing.at[rin_rows(at_tile(j), h)]
         return remote(src, arrived.at[j, core], s_send.at[j, h], s_recv.at[j, core], tile=at_tile(j), arch=pair + h)
 
-    for j in range(1, nt):
+    def block(j):
+        rows = pl.ds(pl.multiple_of(at_tile(j) * fb, 16), fb)
+        outgoing[rows, :] = dot(v[rows, :], scaled).astype(BF16)
+
+    for j in far_first:
+        block(j)
         for h in range(2):
             go(tile_scatter(j, h))
+    block(0)
     go(remote(
         outgoing.at[rin_rows(t, 1 - core)], arrived.at[0, core], s_send.at[0, 0], s_recv.at[0, core], arch=other_core
     ))
@@ -274,7 +280,7 @@
         return dot_last(restored[0], u[0, rows, :]) + dot_last(restored[1], u[1, rows, :])
 
     def lasts(far, side):
-        return tuple(reach if far else reach - (c != side) for c in range(2))
+        return tuple(reach if far else reach - (c % 2 != side) for c in range(nc))
 
     def scatter(step, c, far, side):
         last = lasts(far, side)[c]
@@ -305,7 +311,7 @@
     for far in (0, 1):
         for side in range(2):
             terms = {}
-            for c in range(2):
+            for c in range(nc):
                 m = distance(0, c, far, side)
                 if m not in terms:
                     terms[m] = share(m)
@@ -369,19 +375,19 @@
         sizes = jnp.ones((1, 128), F32)
         for s in range(len_ref.shape[1]):
             sizes = jnp.where(lane == s, len_ref[0, s].astype(F32), sizes)
-        score_ref[...] = total / sizes
+        score_ref[...] = (total / sizes)[:na, : len_ref.shape[1]]
 
     spread()
     for step in range(1, reach):
         for far in (0, 1):
             for side in range(2):
                 terms = {}
-                for c in range(2):
+                for c in range(nc):
                     if step < lasts(far, side)[c]:
                         m = distance(step, c, far, side)
                         if m not in terms:
                             terms[m] = share(m)
-                for c in range(2):
+                for c in range(nc):
                     if step >= lasts(far, side)[c]:
                         continue
                     m = distance(step, c, far, side)
@@ -416,7 +422,7 @@
         sum_tile()
     for side in range(2):
         for h in range(2):
-            for c in range(2):
+            for c in range(nc):
                 slot = final.at[side, h, chunks[c]]
                 remote(slot, slot, r0_send.at[0, side, c], rf_recv.at[side, h, c], grp=z_pair).wait_recv()
     for h in range(2):
@@ -450,6 +456,7 @@
     archive = activations.shape[0]
     ra = archive // nt
     part = fb // 2
+    nc = 2
     reach = nz // 4
     anywhere = pl.BlockSpec(memory_space=pl.ANY)
     dma = pltpu.SemaphoreType.DMA
@@ -457,7 +464,7 @@
     one = dma(())
     pre, scores = pl.pallas_call(
         functools.partial(kernel, nz, nt, na),
-        out_shape=(jax.ShapeDtypeStruct((fb, db), BF16), jax.ShapeDtypeStruct((8, 128), F32)),
+        out_shape=(jax.ShapeDtypeStruct((fb, db), BF16), jax.ShapeDtypeStruct((na, seq_lengths.shape[1]), F32)),
         in_specs=[anywhere] * 6 + [pl.BlockSpec(memory_space=pltpu.SMEM)],
         out_specs=[pl.BlockSpec(memory_space=pltpu.VMEM)] * 2,
         scratch_shapes=[
@@ -488,19 +495,19 @@
             vmem((8, archive), F32),
             vmem((nt, 8, 128), F32),
             vmem((nz, 8, 128), F32),
-            dma((6,)), dma((2, 2, 2)), dma((nz, 2)), dma((nz, 2)), one, one,
+            dma((6,)), dma((2, 2, nc)), dma((nz, nc)), dma((nz, nc)), one, one,
             dma((nz,)), dma((nz,)),
             one, one, dma((nt,)), dma((nt,)), dma((nt,)), dma((nt,)),
             one, one, dma((nt, 2)), dma((nt, 2)), dma((nt,)), dma((nt,)), dma((nt, 2)), dma((nt, 2)),
             one, one, dma((na, 2)), dma((na, 2)),
-            dma((2, 2, 2)), dma((2, 2, reach, 2)), dma((2, 2, reach, 2)), dma((2, 2, 2)), one, one,
+            dma((2, 2, nc)), dma((2, 2, reach, nc)), dma((2, 2, reach, nc)), dma((2, 2, nc)), one, one,
             dma((nt,)), dma((nt,)), dma((nz,)), dma((nz,)),
         ],
         compiler_params=pltpu.CompilerParams(
             collective_id=0, has_side_effects=True, vmem_limit_bytes=60 * 2**20
         ),
     )(query_grads, input_basis, output_basis.T, eigenvalues, activations, gradients.T, seq_lengths)
-    return pre.T[None], scores[:na, : seq_lengths.shape[1]]
+    return pre.T[None], scores
 
 
 def solution(mesh):

time: 97.3 us -> 96.6 us (level)
  Pallas kernels: 93.6 us -> 92.2 us
    pallas_call x1, Pallas kernels: 93.6 us -> 92.2 us  [per_device(): pl.pallas_call(functools.partial(kernel, nz, nt, na), out_shape=(jax.Shap...]
    slice x1 -> x0, local copies, waits for them, and re-layouts: 1.26 us -> none  [per_device(): return (pre.T[None], scores[:na, :seq_lengths.shape[1]])]
    unnamed x1 -> x2, local copies, waits for them, and re-layouts: 1.54 us -> 2.8 us
where the time goes in v4:
time: 96.6 us; the launch traced here: 95.7 us
  Pallas kernels  92.2 us (95%)
  local copies, waits for them, and re-layouts  2.8 us (3%)
    pallas_call x1, Pallas kernels, per_device(): pl.pallas_call(functools.partial(kernel, nz, nt, na), out_shape=(jax.Shap...  92.2 us
    unnamed x2, local copies, waits for them, and re-layouts  2.8 us

profile of v4, /device:TPU:24, one launch (start us, length us, event | category | flops | bytes accessed | tf_op | source)
XLA Modules:
  0.0 95.7 jit_solution(12626077182543441356)
XLA Ops:
  0.6 92.2 %shard_map.86 = (bf16[192,256]{1,0:T(8,128)(2,1)}, f32[4,8]{1,0:T(4,128)}) custom-call(bf16[1,192,256]{2,1,0:T(8,128)(2,1)} %q_hbm.1, bf16[4096,256]{1,0:T(8,128)(2,1)} %u_hbm.1, bf16[192,1536]{1,0:T(8,128)(2,1)} %bitcast.5, f32[192,256]{1,0:T(8,128)} %eig_hbm.1, bf16[256,256]{1,0:T(8,128)(2,1)} %act_hbm.1, bf16[192,256]{1,0:T(8,128)(2,1)} %bitcast.7, ...), custom_call_target="tpu_custom_call" | custom-call | tf_op jit(solution)/shard_map/pallas_call | solution.py:465
  92.9 1.5 %copy.11 = bf16[1,256,192]{1,2,0:T(8,128)(2,1)} copy(bf16[1,256,192]{1,2,0:T(8,128)(2,1)} %bitcast.6) | data formatting | bytes 196608
  94.4 1.3 %copy.12 = f32[4,8]{1,0:T(4,128)} copy(f32[4,8]{1,0:T(4,128)} %get-tuple-element.9) | data formatting | bytes 256

commit v5 on v4

--- a/solution.py
+++ b/solution.py
@@ -139,7 +139,7 @@
             remote(act, acts.at[d], ar_send.at[d], ar_recv.at[d], grp=at_z(d)).wait_recv()
             total += dot(acts[d], u[odd, urows(-d), :])
         aprime[own_rows, :] = total.astype(BF16)
-        for j in range(1, nt):
+        for j in far_first:
             go(remote(aprime.at[own_rows], aprime.at[own_rows], a_send.at[j], a_recv.at[j], tile=at_tile(j)))
 
     def arrive(slot, c):
@@ -193,7 +193,7 @@
             if step == 0:
                 uz_rows = foreign(t, core)
                 remote(uz_rows, uz_rows, uz_send, uz_recv, grp=z_pair).wait_recv()
-                for j in range(1, nt):
+                for j in far_first:
                     go(ut(j))
         for slot in new:
             acc[odd] += dot(pieces[slot], u[odd, urows(slot), :])
@@ -350,7 +350,7 @@
             line = jnp.where(lane == s, one, line)
             start = end
         seq_tile[t] = line
-        for j in range(1, nt):
+        for j in far_first:
             go(remote(seq_tile.at[t], seq_tile.at[t], pt_send.at[j], pt_recv.at[j], tile=at_tile(j)))
 
     def sum_tile():
@@ -361,7 +361,7 @@
         for i in range(1, nt):
             total += seq_tile[i]
         seq_z[z] = total
-        for d in range(1, nz):
+        for d in sorted(range(1, nz), key=lambda k: -min(k, nz - k)):
             go(remote(seq_z.at[z], seq_z.at[z], pz_send.at[d], pz_recv.at[d], grp=at_z(d)))
 
     def sum_z():
@@ -504,7 +504,7 @@
             dma((nt,)), dma((nt,)), dma((nz,)), dma((nz,)),
         ],
         compiler_params=pltpu.CompilerParams(
-            collective_id=0, has_side_effects=True, vmem_limit_bytes=60 * 2**20
+            collective_id=0, has_side_effects=True, vmem_limit_bytes=54 * 2**20
         ),
     )(query_grads, input_basis, output_basis.T, eigenvalues, activations, gradients.T, seq_lengths)
     return pre.T[None], scores

time: 96.6 us -> 95.6 us (0.990)
  Pallas kernels: 92.2 us -> 90.9 us
    pallas_call x1, Pallas kernels: 92.2 us -> 90.9 us  [per_device(): pl.pallas_call(functools.partial(kernel, nz, nt, na), out_shape=(jax.Shap...]
where the time goes in v5:
time: 95.6 us; the launch traced here: 94.3 us
  Pallas kernels  90.9 us (95%)
  local copies, waits for them, and re-layouts  2.8 us (3%)
    pallas_call x1, Pallas kernels, per_device(): pl.pallas_call(functools.partial(kernel, nz, nt, na), out_shape=(jax.Shap...  90.9 us
    unnamed x2, local copies, waits for them, and re-layouts  2.8 us

profile of v5, /device:TPU:24, one launch (start us, length us, event | category | flops | bytes accessed | tf_op | source)
XLA Modules:
  0.0 94.3 jit_solution(2533505181229624940)
XLA Ops:
  0.6 90.9 %shard_map.86 = (bf16[192,256]{1,0:T(8,128)(2,1)}, f32[4,8]{1,0:T(4,128)}) custom-call(bf16[1,192,256]{2,1,0:T(8,128)(2,1)} %q_hbm.1, bf16[4096,256]{1,0:T(8,128)(2,1)} %u_hbm.1, bf16[192,1536]{1,0:T(8,128)(2,1)} %bitcast.5, f32[192,256]{1,0:T(8,128)} %eig_hbm.1, bf16[256,256]{1,0:T(8,128)(2,1)} %act_hbm.1, bf16[192,256]{1,0:T(8,128)(2,1)} %bitcast.7, ...), custom_call_target="tpu_custom_call" | custom-call | tf_op jit(solution)/shard_map/pallas_call | solution.py:465
  91.5 1.5 %copy.11 = bf16[1,256,192]{1,2,0:T(8,128)(2,1)} copy(bf16[1,256,192]{1,2,0:T(8,128)(2,1)} %bitcast.6) | data formatting | bytes 196608
  93.1 1.3 %copy.12 = f32[4,8]{1,0:T(4,128)} copy(f32[4,8]{1,0:T(4,128)} %get-tuple-element.9) | data formatting | bytes 256

commit v6 on v5

--- a/solution.py
+++ b/solution.py
@@ -420,6 +420,9 @@
 
     if reach == 2:
         sum_tile()
+    for copy in sent:
+        copy.wait_send()
+
     for side in range(2):
         for h in range(2):
             for c in range(nc):
@@ -437,8 +440,6 @@
             pre_ref[pl.ds(pl.multiple_of(h * part, 16), part), :] = total.astype(BF16)
 
     sum_z()
-    for copy in sent:
-        copy.wait_send()
 
     @pl.when(same)
     def _():

time: 95.6 us -> 95.4 us (level)
  no operation moved by 1% of the time
where the time goes in v6:
time: 95.4 us; the launch traced here: 94.1 us
  Pallas kernels  90.7 us (95%)
  local copies, waits for them, and re-layouts  2.8 us (3%)
    pallas_call x1, Pallas kernels, per_device(): pl.pallas_call(functools.partial(kernel, nz, nt, na), out_shape=(jax.Shap...  90.7 us
    unnamed x2, local copies, waits for them, and re-layouts  2.8 us

profile of v6, /device:TPU:24, one launch (start us, length us, event | category | flops | bytes accessed | tf_op | source)
XLA Modules:
  0.0 94.1 jit_solution(3290509667300439475)
XLA Ops:
  0.6 90.7 %shard_map.86 = (bf16[192,256]{1,0:T(8,128)(2,1)}, f32[4,8]{1,0:T(4,128)}) custom-call(bf16[1,192,256]{2,1,0:T(8,128)(2,1)} %q_hbm.1, bf16[4096,256]{1,0:T(8,128)(2,1)} %u_hbm.1, bf16[192,1536]{1,0:T(8,128)(2,1)} %bitcast.5, f32[192,256]{1,0:T(8,128)} %eig_hbm.1, bf16[256,256]{1,0:T(8,128)(2,1)} %act_hbm.1, bf16[192,256]{1,0:T(8,128)(2,1)} %bitcast.7, ...), custom_call_target="tpu_custom_call" | custom-call | tf_op jit(solution)/shard_map/pallas_call | solution.py:466
  91.3 1.5 %copy.11 = bf16[1,256,192]{1,2,0:T(8,128)(2,1)} copy(bf16[1,256,192]{1,2,0:T(8,128)(2,1)} %bitcast.6) | data formatting | bytes 196608
  92.8 1.3 %copy.12 = f32[4,8]{1,0:T(4,128)} copy(f32[4,8]{1,0:T(4,128)} %get-tuple-element.9) | data formatting | bytes 256
